TPU v7x, 32 devices: a whole 2x2x4 slice. The times are simulated.
32 devices in a mesh: ka: 8 (over y, x, core), hist: 4 (over z).
Axes of the slice: x: 2, y: 2, z: 4, core: 2. Of those that a mesh axis runs over, the one named last changes fastest.
Arguments:
- green_row: float32 [256, 576, 128], P('hist', 'ka'), may hold values from -6 to 6
- screened: float32 [256, 576, 128], P('hist', 'ka'), may hold values from -0.2 to 0.2
- hamilton: float32 [576, 128], P('ka'), may hold values from -6 to 6
- equal_time: float32 [576, 128], P('ka'), may hold values from -0.5 to 2.5, as said below
- quad_class: int32 [256], P('hist'), may hold values from 0 to 3
- live_count: int32 [4], P('hist'), may hold values from 1 to 64
Outputs:
- green_next: float32 [256, 576, 128], P('hist', 'ka')
Inputs may be any that keep to these rules, and one draw needn't show every extreme that they name: `quad_class`: class c selects the weight q[c] of q = (0.375, 1.1666666, 0.9583333, 1.0). Stored times at positions live_count[j] or later inside block j carry no weight. `equal_time`: the imaginary diagonal entries are positive.
All inputs are finite; a program needn't handle non-finite values.
Results may differ from a plain program's by a relative error of at most 0.00005.
Values sent between devices are 32-bit elements; how exact they have to be, the bound alone decides.
No kernel may reach another device: no remote copies, remote signals or barrier semaphores. Data moves between devices by JAX's collectives and lax.ppermute only.
A program may use at most 64 MiB of HBM per device.

v0:
```python
import functools
import math

import jax
import jax.numpy as jnp
import ml_dtypes
import numpy as np
from jax import lax
from jax.experimental import pallas as pl
from jax.experimental.pallas import tpu as pltpu
from jax.sharding import PartitionSpec as P

SIDE = 24
BANDS = 8
ENTRIES = BANDS * BANDS
WIDTH = 2 * ENTRIES
TILE = 8

time_step = 0.1
hubbard = 1.0
quadrature = (0.375, 1.1666666, 0.9583333, 1.0)

VMEM_LIMIT = 48 * 1024 * 1024


def lane_sign(shape):
    lane = lax.broadcasted_iota(jnp.int32, shape, len(shape) - 1)
    return lane < ENTRIES


def swap(x):
    return pltpu.roll(x, ENTRIES, 1)


def dft24(x, sign, low):
    root3 = jnp.where(low, -1.0, 1.0) * (sign * math.sqrt(3.0) / 2)
    turn = jnp.where(low, -1.0, 1.0) * float(sign)
    half = math.sqrt(0.5)
    turn_half = turn * half
    columns = [[None] * 8 for _ in range(3)]
    for n2 in range(8):
        x0, x1, x2 = (x[(8 * n1 + 3 * n2) % 24] for n1 in range(3))
        total = x1 + x2
        base = x0 - 0.5 * total
        spin = swap(x1 - x2) * root3
        columns[0][n2] = x0 + total
        columns[1][n2] = base + spin
        columns[2][n2] = base - spin
    out = [None] * 24
    for k1 in range(3):
        c = columns[k1]
        a0, a1 = c[0] + c[4], c[0] - c[4]
        a2, a3 = c[2] + c[6], c[2] - c[6]
        a4, a5 = c[1] + c[5], c[1] - c[5]
        a6, a7 = c[3] + c[7], c[3] - c[7]
        b0, b1 = a0 + a2, a0 - a2
        b2, b3 = a4 + a6, a4 - a6
        i_a3 = swap(a3) * turn
        i_b3 = swap(b3) * turn
        c0, c1 = a1 + i_a3, a1 - i_a3
        p = (a5 - a7) * half
        m = swap(a5 + a7) * turn_half
        e, f = p + m, p - m
        values = [b0 + b2, c0 + e, b1 + i_b3, c1 - f, b0 - b2, c0 - e, b1 - i_b3, c1 + f]
        for k2 in range(8):
            out[(16 * k1 + 9 * k2) % 24] = values[k2]
    return out


def first_row(line, block):
    point = line * SIDE
    return (point // block) * (TILE * block) + point % block


def forward_kernel(block, green_ref, lattice_ref, work_ref):
    low = lane_sign((TILE, WIDTH))

    def along_second(k1, carry):
        start = first_row(k1, block)
        rows = [green_ref[pl.ds(start + k2, TILE, stride=block), :] for k2 in range(SIDE)]
        for r2, value in enumerate(dft24(rows, -1, low)):
            work_ref[k1 * SIDE + r2] = value
        return carry

    lax.fori_loop(0, SIDE, along_second, 0)

    def along_first(r2, carry):
        rows = [work_ref[k1 * SIDE + r2] for k1 in range(SIDE)]
        for r1, value in enumerate(dft24(rows, -1, low)):
            lattice_ref[r1 * SIDE + r2] = value
        return carry

    lax.fori_loop(0, SIDE, along_first, 0)


def backward_kernel(
    block, share, lattice_ref, screen_ref, green_ref, weight_ref, equal_ref, gather_ref,
    partial_ref, work_ref, sigma_ref, sums_ref,
):
    points = SIDE * SIDE
    low = lane_sign((TILE, WIDTH))
    turn = jnp.where(low, -1.0, 1.0)
    weights = weight_ref[...]

    def along_second(r1, carry):
        start = first_row(r1, block)
        rows = []
        for r2 in range(SIDE):
            screen = screen_ref[pl.ds(start + r2, TILE, stride=block), :] * weights
            other = swap(screen)
            lattice = lattice_ref[r1 * SIDE + r2]
            rows.append(
                swap(lattice) * turn * jnp.where(low, screen, other)
                - lattice * jnp.where(low, other, screen)
            )
        for k2, value in enumerate(dft24(rows, 1, low)):
            work_ref[r1 * SIDE + k2] = value
        return carry

    lax.fori_loop(0, SIDE, along_second, 0)

    def along_first(k2, carry):
        rows = [work_ref[r1 * SIDE + k2] for r1 in range(SIDE)]
        for k1, value in enumerate(dft24(rows, 1, low)):
            sigma_ref[pl.ds(k1 * SIDE + k2, TILE, stride=points), :] = value
        return carry

    lax.fori_loop(0, SIDE, along_first, 0)

    tiles = block // TILE

    def contract(tile, carry):
        base = (tile // tiles) * (TILE * block) + (tile % tiles) * TILE
        sums = [None] * (2 * BANDS)
        for s in range(TILE):
            sigma = sigma_ref[pl.ds(pl.multiple_of(s * points + tile * TILE, TILE), TILE), :]
            green = green_ref[pl.ds(pl.multiple_of(base + s * block, TILE), TILE), :]
            other = swap(green)
            parts = (jnp.where(low, green, other), jnp.where(low, other, green))
            for d in range(BANDS):
                for h in range(2):
                    part = parts[h] if d == 0 else pltpu.roll(parts[h], WIDTH - BANDS * d, 1)
                    term = sigma * part
                    spot = 2 * d + h
                    sums[spot] = term if s == 0 else sums[spot] + term
        row = pl.ds(pl.multiple_of(tile * TILE, TILE), TILE)
        for spot, value in enumerate(sums):
            sums_ref[row, spot * WIDTH : (spot + 1) * WIDTH] = value
        return carry

    lax.fori_loop(0, points // TILE, contract, 0)

    lane = lax.broadcasted_iota(jnp.int32, equal_ref.shape, 1)
    inner = lane - ENTRIES
    occupied = jnp.sum(jnp.where((inner >= 0) & (inner % (BANDS + 1) == 0), equal_ref[...], 0.0))
    spots = lax.broadcasted_iota(jnp.int32, (points, WIDTH), 1)
    on_diagonal = (spots < ENTRIES) & (spots % (BANDS + 1) == 0)
    sums = sums_ref[...]
    coarse = sums.astype(jnp.bfloat16)
    fine = (sums - coarse.astype(jnp.float32)).astype(jnp.bfloat16)
    gather = gather_ref[...]
    total = jnp.dot(coarse, gather, preferred_element_type=jnp.float32)
    total = total + jnp.dot(fine, gather, preferred_element_type=jnp.float32)
    partial_ref[...] = total + jnp.where(on_diagonal, occupied * share, 0.0)


def propagate_kernel(green_ref, effective_ref, spread_ref, out_ref, factor_ref):
    history, points, _ = green_ref.shape

    @pl.when(pl.program_id(0) == 0)
    def _():
        rest = effective_ref[...] * time_step
        total = None
        for _ in range(3):
            piece = rest.astype(jnp.bfloat16)
            rest = rest - piece.astype(jnp.float32)
            term = jnp.dot(piece, spread_ref[...], preferred_element_type=jnp.float32)
            total = term if total is None else total + term
        factor_ref[...] = total

    for start in range(0, points, TILE):
        stop = min(start + TILE, points)
        low = lane_sign((stop - start, WIDTH))
        factors = [
            factor_ref[start:stop, spot * WIDTH : (spot + 1) * WIDTH] for spot in range(2 * BANDS)
        ]

        def step(s, carry):
            green = green_ref[s, start:stop, :]
            other = swap(green)
            parts = (jnp.where(low, green, other), jnp.where(low, other, green))
            total = green
            for d in range(BANDS):
                for h in range(2):
                    part = parts[h] if d == 0 else pltpu.roll(parts[h], WIDTH - BANDS * d, 1)
                    total = total + factors[2 * d + h] * part
            out_ref[s, start:stop, :] = total
            return carry

        lax.fori_loop(0, history, step, 0, unroll=True)


def gather_table():
    table = np.zeros((2 * BANDS, 2, BANDS, BANDS, 2, BANDS, BANDS), np.float32)
    for d in range(BANDS):
        for a in range(BANDS):
            c = (a + d) % BANDS
            table[2 * d, 0, a, :, 0, a, c] = -1
            table[2 * d, 1, a, :, 1, a, c] = -1
            table[2 * d + 1, 0, a, :, 1, a, c] = 1
            table[2 * d + 1, 1, a, :, 0, a, c] = -1
    return table.reshape(2 * BANDS * WIDTH, WIDTH).astype(ml_dtypes.bfloat16)


def spread_table():
    table = np.zeros((2, BANDS, BANDS, 2 * BANDS, 2, BANDS, BANDS), np.float32)
    for d in range(BANDS):
        for a in range(BANDS):
            b = (a + d) % BANDS
            table[1, a, b, 2 * d, 0, a, :] = 1
            table[0, a, b, 2 * d, 1, a, :] = -1
            table[0, a, b, 2 * d + 1, 0, a, :] = 1
            table[1, a, b, 2 * d + 1, 1, a, :] = 1
    return table.reshape(WIDTH, 2 * BANDS * WIDTH).astype(ml_dtypes.bfloat16)


def forward(green, block):
    points = SIDE * SIDE
    return pl.pallas_call(
        functools.partial(forward_kernel, block),
        out_shape=jax.ShapeDtypeStruct((points, TILE, WIDTH), jnp.float32),
        scratch_shapes=[pltpu.VMEM((points, TILE, WIDTH), jnp.float32)],
        compiler_params=pltpu.CompilerParams(vmem_limit_bytes=VMEM_LIMIT),
        cost_estimate=pl.CostEstimate(
            flops=400 * points * TILE * WIDTH, bytes_accessed=8 * points * TILE * WIDTH, transcendentals=0
        ),
        name="forward",
    )(green)


def backward(lattice, screen, green, weights, equal_time, block, share):
    points = SIDE * SIDE
    return pl.pallas_call(
        functools.partial(backward_kernel, block, share),
        out_shape=jax.ShapeDtypeStruct((points, WIDTH), jnp.float32),
        scratch_shapes=[
            pltpu.VMEM((points, TILE, WIDTH), jnp.float32),
            pltpu.VMEM((TILE * points, WIDTH), jnp.float32),
            pltpu.VMEM((points, 2 * BANDS * WIDTH), jnp.float32),
        ],
        compiler_params=pltpu.CompilerParams(vmem_limit_bytes=VMEM_LIMIT),
        cost_estimate=pl.CostEstimate(
            flops=800 * points * TILE * WIDTH, bytes_accessed=12 * points * TILE * WIDTH, transcendentals=0
        ),
        name="backward",
    )(lattice, screen, green, weights, equal_time, jnp.asarray(gather_table()))


def propagate(greens, effective):
    history, points, width = greens.shape
    step = math.gcd(history, TILE)
    chunk = pl.BlockSpec((step, points, width), lambda i: (i, 0, 0))
    spread = spread_table()
    return pl.pallas_call(
        propagate_kernel,
        grid=(history // step,),
        out_shape=jax.ShapeDtypeStruct(greens.shape, jnp.float32),
        in_specs=[
            chunk,
            pl.BlockSpec((points, width), lambda i: (0, 0)),
            pl.BlockSpec(spread.shape, lambda i: (0, 0)),
        ],
        out_specs=chunk,
        scratch_shapes=[pltpu.VMEM((points, spread.shape[1]), jnp.float32)],
        compiler_params=pltpu.CompilerParams(vmem_limit_bytes=VMEM_LIMIT),
        cost_estimate=pl.CostEstimate(
            flops=32 * greens.size, bytes_accessed=8 * greens.size, transcendentals=0
        ),
        name="propagate",
    )(greens, effective, jnp.asarray(spread))


def class_weights(quad_class):
    table = jnp.array(quadrature, jnp.float32)
    match = quad_class[:, None] == jnp.arange(4, dtype=jnp.int32)[None, :]
    return jnp.sum(jnp.where(match, table[None, :], jnp.float32(0.0)), axis=1)


def per_device(parts, blocks, green_row, screened, hamilton, equal_time, quad_class, live_count):
    history, local, width = green_row.shape
    points = local * parts
    times = history // parts
    moved = [
        lax.all_to_all(x, "ka", split_axis=0, concat_axis=0, tiled=True)
        for x in (green_row, screened)
    ]
    position = jnp.arange(history, dtype=jnp.int32)
    weights = jnp.where(
        position < live_count[0], time_step * class_weights(quad_class), jnp.float32(0.0)
    ) * jnp.float32(1.0 / points)
    weights = lax.dynamic_slice_in_dim(weights, lax.axis_index("ka") * times, times)

    groups = -(-times // TILE)
    if times == TILE and local % SIDE == 0:
        block = local
        moved = [[x.reshape(-1, width)] for x in moved]
    else:
        block = points
        padding = groups * TILE - times
        moved = [
            jnp.pad(
                x.reshape(parts, times, local, width).transpose(1, 0, 2, 3).reshape(times, points, width),
                ((0, padding), (0, 0), (0, 0)),
            ).reshape(groups, TILE * points, width)
            for x in moved
        ]
        weights = jnp.pad(weights, (0, padding))
    weights = jnp.broadcast_to(weights.reshape(groups, TILE, 1), (groups, TILE, width))

    partial_value = None
    for group in range(groups):
        green, screen = moved[0][group], moved[1][group]
        lattice = forward(green, block)
        share = hubbard / (points * blocks) if group == 0 else 0.0
        term = backward(lattice, screen, green, weights[group], equal_time, block, share)
        partial_value = term if partial_value is None else partial_value + term

    collision = lax.psum_scatter(partial_value, "ka", scatter_dimension=0, tiled=True)
    collision = lax.psum(collision, "hist")
    return propagate(green_row, hamilton + collision)


def solution(mesh):
    in_specs = (
        P("hist", "ka", None),
        P("hist", "ka", None),
        P("ka", None),
        P("ka", None),
        P("hist"),
        P("hist"),
    )
    out_specs = P("hist", "ka", None)
    return jax.shard_map(
        functools.partial(per_device, mesh.shape["ka"], mesh.shape["hist"]),
        mesh=mesh,
        in_specs=in_specs,
        out_specs=out_specs,
        check_vma=False,
    )
```

profile of v0, /device:TPU:0, one launch (start us, length us, event | category | flops | bytes accessed | tf_op | source)
XLA Modules:
  0.0 214.9 jit_solution(7421821511547965968)
XLA Ops:
  6.5 34.6 %all_to_all.10 = f32[64,72,128]{2,1,0:T(8,128)S(1)} all-to-all(f32[64,72,128]{2,1,0:T(8,128)} %green_ref.1), channel_id=1, replica_groups=mesh['ka'=8,'hist'=4] {'ka'}, dimensions={0} | all-to-all | bytes 4718592 | tf_op jit(solution)/shard_map/all_to_all | solution.py:294
  41.1 0.0 copy-start
  41.1 0.0 copy-start.8
  41.1 0.0 copy-start.9
  41.1 4.5 %all-to-all-start.1 = ((f32[64,72,128]{2,1,0:T(8,128)}), f32[64,72,128]{2,1,0:T(8,128)}, u32[]{:S(2)}, u32[]{:S(2)}) async-start(f32[64,72,128]{2,1,0:T(8,128)} %param.10), calls=%async_computation.1 | async-start | bytes 4718592 | tf_op jit(solution)/shard_map/all_to_all | solution.py:294
  45.6 0.0 reduce-scatter.4.cloned.1.call-start
  46.3 0.0 copy-done.8
  46.3 0.0 copy-done.9
  46.3 0.1 select_reduce_fusion
  46.4 0.1 dynamic_slice.3
  46.5 0.0 copy-done
  46.5 0.0 copy-start.5
  46.5 0.0 copy-start.6
  46.5 7.4 %forward.1.lattice_ref = f32[576,8,128]{2,1,0:T(8,128)S(1)} custom-call(f32[4608,128]{1,0:T(8,128)S(1)} %bitcast.5), custom_call_target="tpu_custom_call" | custom-call | flops 235929600 | bytes 4718592 | tf_op jit(solution)/shard_map/forward/pallas_call | solution.py:229
  54.0 0.0 copy-start.1
  54.0 1.4 copy-done.1
  55.4 19.7 %all-to-all-done.1 = f32[64,72,128]{2,1,0:T(8,128)} async-done(((f32[64,72,128]{2,1,0:T(8,128)}), f32[64,72,128]{2,1,0:T(8,128)}, u32[]{:S(2)}, u32[]{:S(2)}) %all-to-all-start.1) | async-done | bytes 2359328 | tf_op jit(solution)/shard_map/all_to_all | solution.py:294
  75.1 0.1 squeeze.7.weight_ref
  75.2 0.0 copy-done.5
  75.2 0.0 copy-done.6
  75.2 0.0 copy-start.2
  75.2 1.7 copy-done.2
  76.8 0.0 copy-start.7
  76.8 0.0 copy-start.3
  76.8 0.0 copy-start.4
  76.8 33.9 %backward.1 = f32[576,128]{1,0:T(8,128)} custom-call(f32[576,8,128]{2,1,0:T(8,128)S(1)} %copy-done.2, f32[4608,128]{1,0:T(8,128)} %bitcast.1.screen_ref, f32[4608,128]{1,0:T(8,128)} %bitcast.6, f32[8,128]{1,0:T(8,128)S(1)} %squeeze.7.weight_ref, f32[72,128]{1,0:T(8,128)S(1)} %copy-done.6, bf16[2048,128]{1,0:T(8,128)(2,1)S(1)} %copy-done.5), custom_call_target="tpu_custom_call" | custom-call | flops 471859200 | bytes 7077888 | tf_op jit(solution)/shard_map/backward/pallas_call | solution.py:243
  110.7 0.0 reduce-scatter.4.cloned.1.call-update
  110.7 32.4 %reduce-scatter.4.cloned.1.call-done = f32[72,128]{1,0:T(8,128)} async-done(((f32[576,128]{1,0:T(8,128)}), f32[72,128]{1,0:T(8,128)}) %reduce-scatter.4.cloned.1.call-update) | async-done | bytes 36880
  143.2 19.9 %psum.7 = f32[72,128]{1,0:T(8,128)S(1)} all-reduce(f32[72,128]{1,0:T(8,128)} %reduce-scatter.4.cloned.1.call-done), channel_id=1, replica_groups=mesh['ka'=8,'hist'=4] {'hist'}, use_global_device_ids=true, to_apply=%region_2.3 | all-reduce | flops 9216 | bytes 73728 | tf_op jit(solution)/shard_map/psum | solution.py:329
  163.0 0.0 copy-done.7
  163.1 0.0 copy-done.3
  163.1 0.0 copy-done.4
  163.1 45.0 %propagate.1 = f32[64,72,128]{2,1,0:T(8,128)} custom-call(f32[64,72,128]{2,1,0:T(8,128)S(1)} %copy-done.3, f32[72,128]{1,0:T(8,128)S(1)} %add.11.effective_ref, bf16[128,2048]{1,0:T(8,128)(2,1)S(1)} %copy-done.4), custom_call_target="tpu_custom_call" | custom-call | flops 18874368 | bytes 4718592 | tf_op jit(solution)/shard_map/propagate/pallas_call | solution.py:264
  (2 shorter events, 0.0 us)
Async XLA Ops:
  41.1 5.4 %copy-start = (f32[64,72,128]{2,1,0:T(8,128)}, f32[64,72,128]{2,1,0:T(8,128)S(1)}, u32[]{:S(2)}) copy-start(f32[64,72,128]{2,1,0:T(8,128)S(1)} %all_to_all.10) | copy-start | bytes 7077892
  41.1 5.2 %copy-start.8 = (s32[64]{0:T(128)S(1)}, s32[64]{0:T(128)}, u32[]{:S(2)}) copy-start(s32[64]{0:T(128)} %param.13) | copy-start | bytes 772
  41.1 5.2 %copy-start.9 = (f32[4]{0:T(128)S(1)}, f32[4]{0:T(128)}, u32[]{:S(2)}) copy-start(f32[4]{0:T(128)} %constant.24.clone) | copy-start | bytes 52
  41.1 34.0 %all-to-all-start.1 = ((f32[64,72,128]{2,1,0:T(8,128)}), f32[64,72,128]{2,1,0:T(8,128)}, u32[]{:S(2)}, u32[]{:S(2)}) async-start(f32[64,72,128]{2,1,0:T(8,128)} %param.10), calls=%async_computation.1 | async-start | bytes 4718592 | tf_op jit(solution)/shard_map/all_to_all | solution.py:294
  45.6 97.5 %reduce-scatter.4.cloned.1.call-start = ((), (), s32[]{:S(2)}) async-start(), calls=%async_computation.3 | async-start | bytes 331776
  46.5 28.6 %copy-start.5 = (bf16[2048,128]{1,0:T(8,128)(2,1)S(1)}, bf16[2048,128]{1,0:T(8,128)(2,1)}, u32[]{:S(2)}) copy-start(bf16[2048,128]{1,0:T(8,128)(2,1)} %constant.25.clone.gather_ref) | copy-start | bytes 1572868
  46.5 28.6 %copy-start.6 = (f32[72,128]{1,0:T(8,128)S(1)}, f32[72,128]{1,0:T(8,128)}, u32[]{:S(2)}) copy-start(f32[72,128]{1,0:T(8,128)} %equal_ref.1) | copy-start | bytes 110596
  54.0 1.4 copy-start.1
  75.2 1.7 copy-start.2
  76.8 86.2 %copy-start.7 = (f32[72,128]{1,0:T(8,128)S(1)}, f32[72,128]{1,0:T(8,128)}, u32[]{:S(2)}) copy-start(f32[72,128]{1,0:T(8,128)} %param.11) | copy-start | bytes 110596
  76.8 86.2 %copy-start.3 = (f32[64,72,128]{2,1,0:T(8,128)S(1)}, f32[64,72,128]{2,1,0:T(8,128)}, u32[]{:S(2)}) copy-start(f32[64,72,128]{2,1,0:T(8,128)} %green_ref.1) | copy-start | bytes 7077892
  76.8 86.2 %copy-start.4 = (bf16[128,2048]{1,0:T(8,128)(2,1)S(1)}, bf16[128,2048]{1,0:T(8,128)(2,1)}, u32[]{:S(2)}) copy-start(bf16[128,2048]{1,0:T(8,128)(2,1)} %constant.26.clone.spread_ref) | copy-start | bytes 1572868
Sparse Core Ops, SparseCore 0:
  110.8 32.2 reduce-scatter.3
where the time goes:
time: 215 us
  Pallas kernels  86.3 us (40%)
  blocking collectives  54.4 us (25%)
  waiting for transfers between devices  52.2 us (24%)
  between operations  14.1 us (7%)
  starting transfers between devices  4.54 us (2%)
  local copies, waits for them, and re-layouts  3.24 us (2%)
    pallas_call x1, Pallas kernels, propagate(): pl.pallas_call(propagate_kernel, grid=(history // step,), out_shape=jax.S...  45 us
    all_to_all x1, blocking collectives, per_device(): lax.all_to_all(x, 'ka', split_axis=0, concat_axis=0, tiled=True)  34.6 us
    pallas_call x1, Pallas kernels, backward(): pl.pallas_call(functools.partial(backward_kernel, block, share), out_shap...  33.9 us
    unnamed x2, waiting for transfers between devices  32.5 us
    psum x1, blocking collectives, per_device(): collision = lax.psum(collision, 'hist')  19.9 us
    all_to_all x1, waiting for transfers between devices, per_device(): lax.all_to_all(x, 'ka', split_axis=0, concat_axis=0, tiled=True)  19.7 us
    pallas_call x1, Pallas kernels, forward(): pl.pallas_call(functools.partial(forward_kernel, block), out_shape=jax.Sh...  7.43 us
    all_to_all x1, starting transfers between devices, per_device(): lax.all_to_all(x, 'ka', split_axis=0, concat_axis=0, tiled=True)  4.5 us
  transfers between devices with their start and end apart: 2, of which 2 were waited for; matrix products, arithmetic and copies ran while one was open for 0% of the time, Pallas kernels for 3%

commit v1 on v0

--- a/solution.py
+++ b/solution.py
@@ -30,6 +30,12 @@
 
 def swap(x):
     return pltpu.roll(x, ENTRIES, 1)
+
+
+def tree_sum(terms):
+    while len(terms) > 1:
+        terms = [sum(terms[i : i + 2][1:], terms[i]) for i in range(0, len(terms), 2)]
+    return terms[0]
 
 
 def dft24(x, sign, low):
@@ -94,9 +100,9 @@
 
 
 def backward_kernel(
-    block, share, lattice_ref, screen_ref, green_ref, weight_ref, equal_ref, gather_ref,
-    partial_ref, work_ref, sigma_ref, sums_ref,
+    block, share, place_ref, lattice_ref, screen_ref, green_ref, weight_ref, equal_ref, gather_ref, *rest
 ):
+    *partial_refs, work_ref, sigma_ref, sums_ref = rest
     points = SIDE * SIDE
     low = lane_sign((TILE, WIDTH))
     turn = jnp.where(low, -1.0, 1.0)
@@ -131,21 +137,21 @@
 
     def contract(tile, carry):
         base = (tile // tiles) * (TILE * block) + (tile % tiles) * TILE
-        sums = [None] * (2 * BANDS)
+        sigma, parts = [], []
         for s in range(TILE):
-            sigma = sigma_ref[pl.ds(pl.multiple_of(s * points + tile * TILE, TILE), TILE), :]
+            sigma.append(sigma_ref[pl.ds(pl.multiple_of(s * points + tile * TILE, TILE), TILE), :])
             green = green_ref[pl.ds(pl.multiple_of(base + s * block, TILE), TILE), :]
             other = swap(green)
-            parts = (jnp.where(low, green, other), jnp.where(low, other, green))
-            for d in range(BANDS):
-                for h in range(2):
-                    part = parts[h] if d == 0 else pltpu.roll(parts[h], WIDTH - BANDS * d, 1)
-                    term = sigma * part
-                    spot = 2 * d + h
-                    sums[spot] = term if s == 0 else sums[spot] + term
+            parts.append((jnp.where(low, green, other), jnp.where(low, other, green)))
         row = pl.ds(pl.multiple_of(tile * TILE, TILE), TILE)
-        for spot, value in enumerate(sums):
-            sums_ref[row, spot * WIDTH : (spot + 1) * WIDTH] = value
+        for d in range(BANDS):
+            for h in range(2):
+                terms = [
+                    sigma[s] * (parts[s][h] if d == 0 else pltpu.roll(parts[s][h], WIDTH - BANDS * d, 1))
+                    for s in range(TILE)
+                ]
+                spot = 2 * d + h
+                sums_ref[row, spot * WIDTH : (spot + 1) * WIDTH] = tree_sum(terms)
         return carry
 
     lax.fori_loop(0, points // TILE, contract, 0)
@@ -161,7 +167,11 @@
     gather = gather_ref[...]
     total = jnp.dot(coarse, gather, preferred_element_type=jnp.float32)
     total = total + jnp.dot(fine, gather, preferred_element_type=jnp.float32)
-    partial_ref[...] = total + jnp.where(on_diagonal, occupied * share, 0.0)
+    sigma_ref[:points, :] = total + jnp.where(on_diagonal, occupied * share, 0.0)
+    local = partial_refs[0].shape[0]
+    for step, partial_ref in enumerate(partial_refs):
+        owner = partner_of(place_ref[0], step, len(partial_refs))
+        partial_ref[...] = sigma_ref[pl.ds(owner * local, local), :]
 
 
 def propagate_kernel(green_ref, effective_ref, spread_ref, out_ref, factor_ref):
@@ -178,26 +188,24 @@
             total = term if total is None else total + term
         factor_ref[...] = total
 
-    for start in range(0, points, TILE):
-        stop = min(start + TILE, points)
-        low = lane_sign((stop - start, WIDTH))
-        factors = [
-            factor_ref[start:stop, spot * WIDTH : (spot + 1) * WIDTH] for spot in range(2 * BANDS)
-        ]
-
-        def step(s, carry):
-            green = green_ref[s, start:stop, :]
-            other = swap(green)
-            parts = (jnp.where(low, green, other), jnp.where(low, other, green))
-            total = green
-            for d in range(BANDS):
-                for h in range(2):
-                    part = parts[h] if d == 0 else pltpu.roll(parts[h], WIDTH - BANDS * d, 1)
-                    total = total + factors[2 * d + h] * part
-            out_ref[s, start:stop, :] = total
-            return carry
-
-        lax.fori_loop(0, history, step, 0, unroll=True)
+    def advance(start, stop):
+        low = lane_sign((history, stop - start, WIDTH))
+        green = green_ref[:, start:stop, :]
+        other = pltpu.roll(green, ENTRIES, 2)
+        parts = (jnp.where(low, green, other), jnp.where(low, other, green))
+        terms = [green]
+        for d in range(BANDS):
+            for h in range(2):
+                spot = 2 * d + h
+                factor = factor_ref[start:stop, spot * WIDTH : (spot + 1) * WIDTH]
+                part = parts[h] if d == 0 else pltpu.roll(parts[h], WIDTH - BANDS * d, 2)
+                terms.append(factor[None] * part)
+                if len(terms) == 4:
+                    terms = [tree_sum(terms)]
+        out_ref[:, start:stop, :] = tree_sum(terms)
+
+    for start in range(0, points, 2 * TILE):
+        advance(start, min(start + 2 * TILE, points))
 
 
 def gather_table():
@@ -238,11 +246,14 @@
     )(green)
 
 
-def backward(lattice, screen, green, weights, equal_time, block, share):
+def backward(place, lattice, screen, green, weights, equal_time, block, share, parts):
     points = SIDE * SIDE
+    whole = pl.BlockSpec(memory_space=pltpu.VMEM)
     return pl.pallas_call(
         functools.partial(backward_kernel, block, share),
-        out_shape=jax.ShapeDtypeStruct((points, WIDTH), jnp.float32),
+        out_shape=[jax.ShapeDtypeStruct((points // parts, WIDTH), jnp.float32)] * parts,
+        in_specs=[pl.BlockSpec(memory_space=pltpu.SMEM)] + [whole] * 6,
+        out_specs=[whole] * parts,
         scratch_shapes=[
             pltpu.VMEM((points, TILE, WIDTH), jnp.float32),
             pltpu.VMEM((TILE * points, WIDTH), jnp.float32),
@@ -253,7 +264,7 @@
             flops=800 * points * TILE * WIDTH, bytes_accessed=12 * points * TILE * WIDTH, transcendentals=0
         ),
         name="backward",
-    )(lattice, screen, green, weights, equal_time, jnp.asarray(gather_table()))
+    )(place, lattice, screen, green, weights, equal_time, jnp.asarray(gather_table()))
 
 
 def propagate(greens, effective):
@@ -280,6 +291,17 @@
     )(greens, effective, jnp.asarray(spread))
 
 
+def partner_of(place, step, count):
+    if count & (count - 1) == 0:
+        return place ^ step
+    return (place + step) % count
+
+
+def exchange(value, axis, step, count):
+    pairs = [(place, partner_of(place, step, count)) for place in range(count)]
+    return lax.ppermute(value, axis, pairs)
+
+
 def class_weights(quad_class):
     table = jnp.array(quadrature, jnp.float32)
     match = quad_class[:, None] == jnp.arange(4, dtype=jnp.int32)[None, :]
@@ -317,16 +339,23 @@
         weights = jnp.pad(weights, (0, padding))
     weights = jnp.broadcast_to(weights.reshape(groups, TILE, 1), (groups, TILE, width))
 
-    partial_value = None
+    place = lax.axis_index("ka")
+    pieces = None
     for group in range(groups):
         green, screen = moved[0][group], moved[1][group]
         lattice = forward(green, block)
         share = hubbard / (points * blocks) if group == 0 else 0.0
-        term = backward(lattice, screen, green, weights[group], equal_time, block, share)
-        partial_value = term if partial_value is None else partial_value + term
-
-    collision = lax.psum_scatter(partial_value, "ka", scatter_dimension=0, tiled=True)
-    collision = lax.psum(collision, "hist")
+        terms = backward(
+            place.reshape(1), lattice, screen, green, weights[group], equal_time, block, share, parts
+        )
+        pieces = list(terms) if pieces is None else [a + b for a, b in zip(pieces, terms)]
+
+    partial_value = tree_sum(
+        pieces[:1] + [exchange(pieces[step], "ka", step, parts) for step in range(1, parts)]
+    )
+    collision = tree_sum(
+        [partial_value] + [exchange(partial_value, "hist", step, blocks) for step in range(1, blocks)]
+    )
     return propagate(green_row, hamilton + collision)
 
 

time: 215 us -> 135 us (0.63)
  Pallas kernels: 86.3 us -> 53.9 us
  waiting for transfers between devices: 52.2 us -> 26.8 us
  blocking collectives: 54.4 us -> 34.6 us
  between operations: 14.1 us -> 0.74 us
  starting transfers between devices: 4.54 us -> 15.1 us
    unnamed x2 -> x0, waiting for transfers between devices: 32.5 us -> none
    pallas_call x1, Pallas kernels: 45 us -> 13 us  [propagate(): pl.pallas_call(propagate_kernel, grid=(history // step,), out_shape=jax.S...]
    psum x1 -> x0, blocking collectives: 19.9 us -> none  [per_device(): collision = lax.psum(collision, 'hist')]
    ppermute x0 -> x10, starting transfers between devices: none -> 10.6 us  [exchange(): return lax.ppermute(value, axis, pairs)]
    ppermute x0 -> x10, waiting for transfers between devices: none -> 7.03 us  [exchange(): return lax.ppermute(value, axis, pairs)]
  transfers between devices with their start and end apart: 2 -> 11, of which waited for: 2 -> 6; matrix products, arithmetic and copies ran while one was open for 0% -> 0% of each run, Pallas kernels for 3% -> 6%
where the time goes in v1:
time: 135 us; the launch traced here: 134 us
  Pallas kernels  53.9 us (40%)
  blocking collectives  34.6 us (26%)
  waiting for transfers between devices  26.8 us (20%)
  starting transfers between devices  15.1 us (11%)
  local copies, waits for them, and re-layouts  3.24 us (2%)
    all_to_all x1, blocking collectives, per_device(): lax.all_to_all(x, 'ka', split_axis=0, concat_axis=0, tiled=True)  34.6 us
    pallas_call x1, Pallas kernels, backward(): pl.pallas_call(functools.partial(backward_kernel, block, share), out_shap...  33.4 us
    all_to_all x1, waiting for transfers between devices, per_device(): lax.all_to_all(x, 'ka', split_axis=0, concat_axis=0, tiled=True)  19.8 us
    pallas_call x1, Pallas kernels, propagate(): pl.pallas_call(propagate_kernel, grid=(history // step,), out_shape=jax.S...  13 us
    ppermute x10, starting transfers between devices, exchange(): return lax.ppermute(value, axis, pairs)  10.6 us
    pallas_call x1, Pallas kernels, forward(): pl.pallas_call(functools.partial(forward_kernel, block), out_shape=jax.Sh...  7.43 us
    ppermute x10, waiting for transfers between devices, exchange(): return lax.ppermute(value, axis, pairs)  7.03 us
    all_to_all x1, starting transfers between devices, per_device(): lax.all_to_all(x, 'ka', split_axis=0, concat_axis=0, tiled=True)  4.5 us
  transfers between devices with their start and end apart: 11, of which 6 were waited for; matrix products, arithmetic and copies ran while one was open for 0% of the time, Pallas kernels for 6%

profile of v1, /device:TPU:0, one launch (start us, length us, event | category | flops | bytes accessed | tf_op | source)
XLA Modules:
  0.0 134.4 jit_solution(13925906455201967774)
XLA Ops:
  0.0 34.6 %all_to_all.10 = f32[64,72,128]{2,1,0:T(8,128)S(1)} all-to-all(f32[64,72,128]{2,1,0:T(8,128)} %green_ref.1), channel_id=1, replica_groups=mesh['ka'=8,'hist'=4] {'ka'}, dimensions={0} | all-to-all | bytes 4718592 | tf_op jit(solution)/shard_map/all_to_all | solution.py:316
  34.6 0.0 copy-start
  34.6 0.0 copy-start.8
  34.6 0.0 copy-start.9
  34.6 4.5 %all-to-all-start.1 = ((f32[64,72,128]{2,1,0:T(8,128)}), f32[64,72,128]{2,1,0:T(8,128)}, u32[]{:S(2)}, u32[]{:S(2)}) async-start(f32[64,72,128]{2,1,0:T(8,128)} %param.10), calls=%async_computation.1 | async-start | bytes 4718592 | tf_op jit(solution)/shard_map/all_to_all | solution.py:316
  39.7 0.0 copy-done.8
  39.8 0.0 copy-done.9
  39.8 0.1 select_reduce_fusion
  39.9 0.1 dynamic_slice.3
  39.9 0.0 copy-done
  39.9 0.0 copy-start.5
  39.9 0.0 copy-start.6
  39.9 7.4 %forward.1.lattice_ref = f32[576,8,128]{2,1,0:T(8,128)S(1)} custom-call(f32[4608,128]{1,0:T(8,128)S(1)} %bitcast.5), custom_call_target="tpu_custom_call" | custom-call | flops 235929600 | bytes 4718592 | tf_op jit(solution)/shard_map/forward/pallas_call | solution.py:237
  47.4 0.0 copy-start.1
  47.4 1.4 %copy-done.1 = f32[576,8,128]{2,1,0:T(8,128)} copy-done((f32[576,8,128]{2,1,0:T(8,128)}, f32[576,8,128]{2,1,0:T(8,128)S(1)}, u32[]{:S(2)}) %copy-start.1) | copy-done | bytes 2359320
  48.8 19.8 %all-to-all-done.1 = f32[64,72,128]{2,1,0:T(8,128)} async-done(((f32[64,72,128]{2,1,0:T(8,128)}), f32[64,72,128]{2,1,0:T(8,128)}, u32[]{:S(2)}, u32[]{:S(2)}) %all-to-all-start.1) | async-done | bytes 2359328 | tf_op jit(solution)/shard_map/all_to_all | solution.py:316
  68.6 0.1 squeeze.7.weight_ref
  68.6 0.0 copy-done.5
  68.6 0.0 copy-done.6
  68.6 0.0 copy-start.2
  68.6 1.7 %copy-done.2 = f32[576,8,128]{2,1,0:T(8,128)S(1)} copy-done((f32[576,8,128]{2,1,0:T(8,128)S(1)}, f32[576,8,128]{2,1,0:T(8,128)}, u32[]{:S(2)}) %copy-start.2) | copy-done | bytes 2359320
  70.3 0.0 copy-start.3
  70.3 0.0 copy-start.4
  70.3 33.4 %backward.1 = (f32[72,128]{1,0:T(8,128)S(1)}, f32[72,128]{1,0:T(8,128)S(1)}, f32[72,128]{1,0:T(8,128)S(1)}, f32[72,128]{1,0:T(8,128)S(1)}, f32[72,128]{1,0:T(8,1...) custom-call(s32[1]{0:T(128)} %bitcast.place_ref, f32[576,8,128]{2,1,0:T(8,128)S(1)} %copy-done.2, ...), custom_call_target="tpu_custom_call" | custom-call | flops 471859200 | bytes 7077888 | tf_op jit(solution)/shard_map/backward/pallas_call | solution.py:252
  103.7 0.1 collective-permute-start
  103.8 0.6 collective-permute-start.1
  104.4 1.3 collective-permute-start.2
  105.7 0.5 collective-permute-start.3
  106.2 1.1 collective-permute-start.4
  107.4 0.0 collective-permute-done
  107.4 0.6 collective-permute-start.5
  107.9 0.2 collective-permute-done.1
  108.1 1.9 %collective-permute-start.6 = (f32[72,128]{1,0:T(8,128)S(1)}, f32[72,128]{1,0:T(8,128)S(1)}, u32[]{:S(2)}, u32[]{:S(2)}) collective-permute-start(f32[72,128]{1,0:T(8,128)S(1)} %get-tuple-element.20), channel_id=1, source_target_pairs={{0,28},{4,24},{8,20},{12,16},{16,12},{20,8},{24,4},{28,0},{1,29},{... | collective-permute-start | bytes 110600 | tf_op jit(solution)/shard_map/ppermute | solution.py:302
  110.1 0.0 collective-permute-done.2
  110.1 0.0 collective-permute-done.3
  110.1 0.0 collective-permute-done.4
  110.1 2.3 %collective-permute-done.5 = f32[72,128]{1,0:T(8,128)S(1)} collective-permute-done((f32[72,128]{1,0:T(8,128)S(1)}, f32[72,128]{1,0:T(8,128)S(1)}, u32[]{:S(2)}, u32[]{:S(2)}) %collective-permute-start.5) | collective-permute-done | bytes 36896 | tf_op jit(solution)/shard_map/ppermute | solution.py:302
  112.4 0.4 collective-permute-done.6
  112.8 3.7 %collective-permute-start.9 = (f32[72,128]{1,0:T(8,128)S(1)}, f32[72,128]{1,0:T(8,128)S(1)}, u32[]{:S(2)}, u32[]{:S(2)}) collective-permute-start(f32[72,128]{1,0:T(8,128)S(1)} %add_add_fusion.1), channel_id=1, source_target_pairs={{0,3},{1,2},{2,1},{3,0},{4,7},{5,6},{6,5},{7,4},{8,11},{9,10},{10,... | collective-permute-start | bytes 110600 | tf_op jit(solution)/shard_map/ppermute | solution.py:302
  116.5 0.0 collective-permute-start.8
  116.5 0.8 collective-permute-start.7
  117.3 1.4 %collective-permute-done.9 = f32[72,128]{1,0:T(8,128)S(1)} collective-permute-done((f32[72,128]{1,0:T(8,128)S(1)}, f32[72,128]{1,0:T(8,128)S(1)}, u32[]{:S(2)}, u32[]{:S(2)}) %collective-permute-start.9) | collective-permute-done | bytes 36896 | tf_op jit(solution)/shard_map/ppermute | solution.py:302
  118.7 2.7 %collective-permute-done.8 = f32[72,128]{1,0:T(8,128)S(1)} collective-permute-done((f32[72,128]{1,0:T(8,128)S(1)}, f32[72,128]{1,0:T(8,128)S(1)}, u32[]{:S(2)}, u32[]{:S(2)}) %collective-permute-start.8) | collective-permute-done | bytes 36896 | tf_op jit(solution)/shard_map/ppermute | solution.py:302
  121.4 0.0 collective-permute-done.7
  121.4 0.0 copy-done.7
  121.4 0.0 copy-done.3
  121.4 0.0 copy-done.4
  121.4 13.0 %propagate.1 = f32[64,72,128]{2,1,0:T(8,128)} custom-call(f32[64,72,128]{2,1,0:T(8,128)S(1)} %copy-done.3, f32[72,128]{1,0:T(8,128)S(1)} %add_add_fusion.effective_ref, bf16[128,2048]{1,0:T(8,128)(2,1)S(1)} %copy-done.4), custom_call_target="tpu_custom_call" | custom-call | flops 18874368 | bytes 4718592 | tf_op jit(solution)/shard_map/propagate/pallas_call | solution.py:275
  (4 shorter events, 0.0 us)
Async XLA Ops:
  34.6 5.4 %copy-start = (f32[64,72,128]{2,1,0:T(8,128)}, f32[64,72,128]{2,1,0:T(8,128)S(1)}, u32[]{:S(2)}) copy-start(f32[64,72,128]{2,1,0:T(8,128)S(1)} %all_to_all.10) | copy-start | bytes 7077892
  34.6 5.2 %copy-start.8 = (s32[64]{0:T(128)S(1)}, s32[64]{0:T(128)}, u32[]{:S(2)}) copy-start(s32[64]{0:T(128)} %param.13) | copy-start | bytes 772
  34.6 5.2 %copy-start.9 = (f32[4]{0:T(128)S(1)}, f32[4]{0:T(128)}, u32[]{:S(2)}) copy-start(f32[4]{0:T(128)} %constant.24.clone) | copy-start | bytes 52
  34.6 34.0 %all-to-all-start.1 = ((f32[64,72,128]{2,1,0:T(8,128)}), f32[64,72,128]{2,1,0:T(8,128)}, u32[]{:S(2)}, u32[]{:S(2)}) async-start(f32[64,72,128]{2,1,0:T(8,128)} %param.10), calls=%async_computation.1 | async-start | bytes 4718592 | tf_op jit(solution)/shard_map/all_to_all | solution.py:316
  39.9 28.7 %copy-start.5 = (bf16[2048,128]{1,0:T(8,128)(2,1)S(1)}, bf16[2048,128]{1,0:T(8,128)(2,1)}, u32[]{:S(2)}) copy-start(bf16[2048,128]{1,0:T(8,128)(2,1)} %constant.25.clone.gather_ref) | copy-start | bytes 1572868
  39.9 28.7 %copy-start.6 = (f32[72,128]{1,0:T(8,128)S(1)}, f32[72,128]{1,0:T(8,128)}, u32[]{:S(2)}) copy-start(f32[72,128]{1,0:T(8,128)} %equal_ref.1) | copy-start | bytes 110596
  47.4 1.4 %copy-start.1 = (f32[576,8,128]{2,1,0:T(8,128)}, f32[576,8,128]{2,1,0:T(8,128)S(1)}, u32[]{:S(2)}) copy-start(f32[576,8,128]{2,1,0:T(8,128)S(1)} %forward.1.lattice_ref) | copy-start | bytes 7077892
  68.6 1.7 %copy-start.2 = (f32[576,8,128]{2,1,0:T(8,128)S(1)}, f32[576,8,128]{2,1,0:T(8,128)}, u32[]{:S(2)}) copy-start(f32[576,8,128]{2,1,0:T(8,128)} %copy-done.1) | copy-start | bytes 7077892
  70.3 51.1 %copy-start.7 = (f32[72,128]{1,0:T(8,128)S(1)}, f32[72,128]{1,0:T(8,128)}, u32[]{:S(2)}) copy-start(f32[72,128]{1,0:T(8,128)} %param.11) | copy-start | bytes 110596
  70.3 51.1 %copy-start.3 = (f32[64,72,128]{2,1,0:T(8,128)S(1)}, f32[64,72,128]{2,1,0:T(8,128)}, u32[]{:S(2)}) copy-start(f32[64,72,128]{2,1,0:T(8,128)} %green_ref.1) | copy-start | bytes 7077892
  70.3 51.1 %copy-start.4 = (bf16[128,2048]{1,0:T(8,128)(2,1)S(1)}, bf16[128,2048]{1,0:T(8,128)(2,1)}, u32[]{:S(2)}) copy-start(bf16[128,2048]{1,0:T(8,128)(2,1)} %constant.26.clone.spread_ref) | copy-start | bytes 1572868
  103.7 3.6 %collective-permute-start = (f32[72,128]{1,0:T(8,128)S(1)}, f32[72,128]{1,0:T(8,128)S(1)}, u32[]{:S(2)}, u32[]{:S(2)}) collective-permute-start(f32[72,128]{1,0:T(8,128)S(1)} %get-tuple-element.14), channel_id=1, source_target_pairs={{0,4},{4,0},{8,12},{12,8},{16,20},{20,16},{24,28},{28,24},{1,5},{5... | collective-permute-start | bytes 110600 | tf_op jit(solution)/shard_map/ppermute | solution.py:302
  103.8 4.3 %collective-permute-start.1 = (f32[72,128]{1,0:T(8,128)S(1)}, f32[72,128]{1,0:T(8,128)S(1)}, u32[]{:S(2)}, u32[]{:S(2)}) collective-permute-start(f32[72,128]{1,0:T(8,128)S(1)} %get-tuple-element.15), channel_id=1, source_target_pairs={{0,8},{4,12},{8,0},{12,4},{16,24},{20,28},{24,16},{28,20},{1,9},{5... | collective-permute-start | bytes 110600 | tf_op jit(solution)/shard_map/ppermute | solution.py:302
  104.4 5.7 %collective-permute-start.2 = (f32[72,128]{1,0:T(8,128)S(1)}, f32[72,128]{1,0:T(8,128)S(1)}, u32[]{:S(2)}, u32[]{:S(2)}) collective-permute-start(f32[72,128]{1,0:T(8,128)S(1)} %get-tuple-element.16), channel_id=1, source_target_pairs={{0,12},{4,8},{8,4},{12,0},{16,28},{20,24},{24,20},{28,16},{1,13},{... | collective-permute-start | bytes 110600 | tf_op jit(solution)/shard_map/ppermute | solution.py:302
  105.7 4.4 %collective-permute-start.3 = (f32[72,128]{1,0:T(8,128)S(1)}, f32[72,128]{1,0:T(8,128)S(1)}, u32[]{:S(2)}, u32[]{:S(2)}) collective-permute-start(f32[72,128]{1,0:T(8,128)S(1)} %get-tuple-element.17), channel_id=1, source_target_pairs={{0,16},{4,20},{8,24},{12,28},{16,0},{20,4},{24,8},{28,12},{1,17},{... | collective-permute-start | bytes 110600 | tf_op jit(solution)/shard_map/ppermute | solution.py:302
  106.2 3.9 %collective-permute-start.4 = (f32[72,128]{1,0:T(8,128)S(1)}, f32[72,128]{1,0:T(8,128)S(1)}, u32[]{:S(2)}, u32[]{:S(2)}) collective-permute-start(f32[72,128]{1,0:T(8,128)S(1)} %get-tuple-element.18), channel_id=1, source_target_pairs={{0,20},{4,16},{8,28},{12,24},{16,4},{20,0},{24,12},{28,8},{1,21},{... | collective-permute-start | bytes 110600 | tf_op jit(solution)/shard_map/ppermute | solution.py:302
  107.4 5.0 %collective-permute-start.5 = (f32[72,128]{1,0:T(8,128)S(1)}, f32[72,128]{1,0:T(8,128)S(1)}, u32[]{:S(2)}, u32[]{:S(2)}) collective-permute-start(f32[72,128]{1,0:T(8,128)S(1)} %get-tuple-element.19), channel_id=1, source_target_pairs={{0,24},{4,28},{8,16},{12,20},{16,8},{20,12},{24,0},{28,4},{1,25},{... | collective-permute-start | bytes 110600 | tf_op jit(solution)/shard_map/ppermute | solution.py:302
  108.1 4.7 %collective-permute-start.6 = (f32[72,128]{1,0:T(8,128)S(1)}, f32[72,128]{1,0:T(8,128)S(1)}, u32[]{:S(2)}, u32[]{:S(2)}) collective-permute-start(f32[72,128]{1,0:T(8,128)S(1)} %get-tuple-element.20), channel_id=1, source_target_pairs={{0,28},{4,24},{8,20},{12,16},{16,12},{20,8},{24,4},{28,0},{1,29},{... | collective-permute-start | bytes 110600 | tf_op jit(solution)/shard_map/ppermute | solution.py:302
  112.8 5.8 %collective-permute-start.9 = (f32[72,128]{1,0:T(8,128)S(1)}, f32[72,128]{1,0:T(8,128)S(1)}, u32[]{:S(2)}, u32[]{:S(2)}) collective-permute-start(f32[72,128]{1,0:T(8,128)S(1)} %add_add_fusion.1), channel_id=1, source_target_pairs={{0,3},{1,2},{2,1},{3,0},{4,7},{5,6},{6,5},{7,4},{8,11},{9,10},{10,... | collective-permute-start | bytes 110600 | tf_op jit(solution)/shard_map/ppermute | solution.py:302
  116.5 4.9 %collective-permute-start.8 = (f32[72,128]{1,0:T(8,128)S(1)}, f32[72,128]{1,0:T(8,128)S(1)}, u32[]{:S(2)}, u32[]{:S(2)}) collective-permute-start(f32[72,128]{1,0:T(8,128)S(1)} %add_add_fusion.1), channel_id=1, source_target_pairs={{0,2},{1,3},{2,0},{3,1},{4,6},{5,7},{6,4},{7,5},{8,10},{9,11},{10,... | collective-permute-start | bytes 110600 | tf_op jit(solution)/shard_map/ppermute | solution.py:302
  116.5 4.9 %collective-permute-start.7 = (f32[72,128]{1,0:T(8,128)S(1)}, f32[72,128]{1,0:T(8,128)S(1)}, u32[]{:S(2)}, u32[]{:S(2)}) collective-permute-start(f32[72,128]{1,0:T(8,128)S(1)} %add_add_fusion.1), channel_id=1, source_target_pairs={{0,1},{1,0},{2,3},{3,2},{4,5},{5,4},{6,7},{7,6},{8,9},{9,8},{10,11... | collective-permute-start | bytes 110600 | tf_op jit(solution)/shard_map/ppermute | solution.py:302
